TPU v7x, 128 devices: a whole 4x4x4 slice. The times are simulated.
128 devices in a mesh: seq: 32 (over x, z, y_hi), proj: 4 (over y_lo, core).
Axes of the slice: x: 4, y: 4 (y_hi: 2, y_lo: 2; y = y_hi * 2 + y_lo), z: 4, core: 2. Of those that a mesh axis runs over, the one named last changes fastest.
Arguments:
- tokens: bfloat16 [8192, 8192], P('seq', 'proj'), may hold values from -6 to 6
- value_weight: bfloat16 [8192, 4096], P('proj'), may hold values from -0.0625 to 0.0625
- query: bfloat16 [8192, 4096], P('seq', 'proj'), may hold values from -6 to 6
- keyed: bfloat16 [8192, 4096], P('seq', 'proj'), may hold values from -6 to 6
- filters: float32 [8192, 4096], P('seq', 'proj'), may hold values from -2 to 2
- skip_gain: float32 [4096], P('proj'), may hold values from -4 to 4
Outputs:
- mixed_out: bfloat16 [8192, 4096], P('seq', 'proj')
All inputs are finite; a program needn't handle non-finite values.
Results may differ from a plain program's by a relative error of at most 0.0017.
Values sent between devices are 32-bit elements; how exact they have to be, the bound alone decides.
A program may use at most 128 MiB of HBM per device.

v0:
```python
import math

import jax
import jax.numpy as jnp
from jax import lax
from jax.sharding import PartitionSpec as P

HIGHEST = lax.Precision.HIGHEST


def from_partner(block, axis, stride):
    count = lax.axis_size(axis)
    route = []
    for low in range(count):
        high = low | 1 << stride
        if high != low and high < count:
            route += [(low, high), (high, low)]
    return lax.ppermute(block, axis, route)


def angle_table(first, second, modulus):
    product = first[:, None] * second[None, :] % modulus
    angles = 2.0 * math.pi / modulus * product.astype(jnp.float32)
    return (jnp.cos(angles), jnp.sin(angles))


def rotate(real_part, imag_part, cosine, sine, sign):
    return (
        real_part * cosine - sign * imag_part * sine,
        imag_part * cosine + sign * real_part * sine,
    )


def local_dft(real_part, imag_part, sign):
    size = real_part.shape[1]
    index = jnp.arange(size, dtype=jnp.int32)
    cosine, sine = angle_table(index, index, size)

    def apply_table(table, values):
        return jnp.einsum("kj,ejc->ekc", table, values, precision=HIGHEST)

    return (
        apply_table(cosine, real_part) - sign * apply_table(sine, imag_part),
        apply_table(cosine, imag_part) + sign * apply_table(sine, real_part),
    )


def spectral_product(spec_real, spec_imag, width):
    freq_real, freq_imag = local_dft(spec_real, spec_imag, -1.0)
    data_real, filt_real = (freq_real[:, :, :width], freq_real[:, :, width:])
    data_imag, filt_imag = (freq_imag[:, :, :width], freq_imag[:, :, width:])
    prod_real = data_real * filt_real - data_imag * filt_imag
    prod_imag = data_real * filt_imag + data_imag * filt_real
    return local_dft(prod_real, prod_imag, 1.0)


def by_pairs(gated, filters, seq_count, seq_index):
    blk_rows, width = gated.shape
    modulus = 2 * blk_rows * seq_count
    level_count = seq_count.bit_length() - 1
    seq_float = seq_index.astype(jnp.float32)
    signal = jnp.concatenate([gated, filters], axis=1)
    pair_base = jnp.arange(2, dtype=jnp.int32)
    all_positions = jnp.arange(blk_rows, dtype=jnp.int32)
    half_cos = jnp.cos(math.pi * seq_float / seq_count)
    half_sin = jnp.sin(math.pi * seq_float / seq_count)
    spec_real = jnp.stack([signal, signal * half_cos])
    spec_imag = jnp.stack([jnp.zeros_like(signal), -signal * half_sin])
    for level in reversed(range(level_count)):
        stride = 1 << level
        other_real, other_imag = from_partner((spec_real, spec_imag), "seq", level)
        upper_half = seq_index // stride % 2 == 1
        step_angle = math.pi * (seq_index % stride).astype(jnp.float32) / stride
        rot_real, rot_imag = rotate(
            other_real - spec_real,
            other_imag - spec_imag,
            jnp.cos(step_angle),
            jnp.sin(step_angle),
            -1.0,
        )
        spec_real = jnp.where(upper_half, rot_real, spec_real + other_real)
        spec_imag = jnp.where(upper_half, rot_imag, spec_imag + other_imag)
    reversed_index = jnp.zeros((), jnp.int32)
    for level in range(level_count):
        reversed_index = reversed_index + seq_index // (1 << level) % 2 * (
            1 << level_count - 1 - level
        )
    own_freq = 2 * reversed_index + pair_base
    tw_cos, tw_sin = angle_table(own_freq, all_positions, modulus)
    spec_real, spec_imag = rotate(
        spec_real, spec_imag, tw_cos[:, :, None], tw_sin[:, :, None], -1.0
    )
    back_real, back_imag = spectral_product(spec_real, spec_imag, width)
    back_real, back_imag = rotate(back_real, back_imag, tw_cos[:, :, None], tw_sin[:, :, None], 1.0)
    for level in range(level_count):
        stride = 1 << level
        other_real, other_imag = from_partner((back_real, back_imag), "seq", level)
        upper_half = seq_index // stride % 2 == 1
        step_angle = math.pi * (seq_index % stride).astype(jnp.float32) / stride
        step_cos = jnp.cos(step_angle)
        step_sin = jnp.sin(step_angle)
        other_rot_r, other_rot_i = rotate(other_real, other_imag, step_cos, step_sin, 1.0)
        own_rot_r, own_rot_i = rotate(back_real, back_imag, step_cos, step_sin, 1.0)
        back_real = jnp.where(upper_half, other_real - own_rot_r, back_real + other_rot_r)
        back_imag = jnp.where(upper_half, other_imag - own_rot_i, back_imag + other_rot_i)
    return (back_real[0] + half_cos * back_real[1] - half_sin * back_imag[1]) / modulus


def body(tokens, value_weight, query, keyed, filters, skip_gain):
    seq_count = lax.axis_size("seq")
    seq_index = lax.axis_index("seq")
    partial_value = jnp.dot(tokens, value_weight, preferred_element_type=jnp.float32)
    valued = lax.psum_scatter(partial_value, "proj", scatter_dimension=1, tiled=True)
    gated = keyed.astype(jnp.float32) * valued
    conv = by_pairs(gated, filters, seq_count, seq_index)
    return (query.astype(jnp.float32) * (conv + skip_gain * gated)).astype(jnp.bfloat16)


def solution(mesh):
    in_specs = (
        P("seq", "proj"),
        P("proj", None),
        P("seq", "proj"),
        P("seq", "proj"),
        P("seq", "proj"),
        P("proj"),
    )
    out_specs = P("seq", "proj")
    return jax.shard_map(body, mesh=mesh, in_specs=in_specs, out_specs=out_specs, check_vma=False)
```

profile of v0, /device:TPU:0, one launch (start us, length us, event | category | flops | bytes accessed | tf_op | source)
XLA Modules:
  0.0 1533.1 jit_solution(8932063419584621738)
XLA Ops:
  7.8 10.1 fusion.81
  18.1 47.8 %reduce-scatter.2.cloned.1.call-done = f32[256,1024]{1,0:T(8,128)} async-done(((f32[256,4096]{1,0:T(8,128)}), f32[256,1024]{1,0:T(8,128)}) %reduce-scatter.2.cloned.1.call-update) | async-done | bytes 1048592 | tf_op jit(solution)/shard_map/reduce_scatter | solution.py:113
  69.8 2.5 pad_maximum_fusion
  72.5 3.0 collective-permute-start
  75.5 2.5 stack.13
  78.7 89.0 %collective-permute-done = f32[2,256,2048]{2,1,0:T(8,128)} collective-permute-done((f32[2,256,2048]{2,1,0:T(8,128)}, f32[2,256,2048]{2,1,0:T(8,128)}, u32[]{:S(2)}, u32[]{:S(2)}) %collective-permute-start) | collective-permute-done | bytes 4194336 | tf_op jit(solution)/shard_map/ppermute | solution.py:18
  167.7 89.0 %collective-permute-done.1 = f32[2,256,2048]{2,1,0:T(8,128)} collective-permute-done((f32[2,256,2048]{2,1,0:T(8,128)}, f32[2,256,2048]{2,1,0:T(8,128)}, u32[]{:S(2)}, u32[]{:S(2)}) %collective-permute-start.1) | collective-permute-done | bytes 4194336 | tf_op jit(solution)/shard_map/ppermute | solution.py:18
  256.8 7.8 add_select_fusion.9
  266.7 91.6 %collective-permute-done.2 = f32[2,256,2048]{2,1,0:T(8,128)} collective-permute-done((f32[2,256,2048]{2,1,0:T(8,128)}, f32[2,256,2048]{2,1,0:T(8,128)}, u32[]{:S(2)}, u32[]{:S(2)}) %collective-permute-start.2) | collective-permute-done | bytes 4194336 | tf_op jit(solution)/shard_map/ppermute | solution.py:18
  358.4 88.1 %collective-permute-done.3 = f32[2,256,2048]{2,1,0:T(8,128)} collective-permute-done((f32[2,256,2048]{2,1,0:T(8,128)}, f32[2,256,2048]{2,1,0:T(8,128)}, u32[]{:S(2)}, u32[]{:S(2)}) %collective-permute-start.3) | collective-permute-done | bytes 4194336 | tf_op jit(solution)/shard_map/ppermute | solution.py:18
  446.5 9.2 add_select_fusion.7
  455.7 3.1 collective-permute-start.4
  459.4 91.6 %collective-permute-done.4 = f32[2,256,2048]{2,1,0:T(8,128)} collective-permute-done((f32[2,256,2048]{2,1,0:T(8,128)}, f32[2,256,2048]{2,1,0:T(8,128)}, u32[]{:S(2)}, u32[]{:S(2)}) %collective-permute-start.4) | collective-permute-done | bytes 4194336 | tf_op jit(solution)/shard_map/ppermute | solution.py:18
  551.0 87.2 %collective-permute-done.5 = f32[2,256,2048]{2,1,0:T(8,128)} collective-permute-done((f32[2,256,2048]{2,1,0:T(8,128)}, f32[2,256,2048]{2,1,0:T(8,128)}, u32[]{:S(2)}, u32[]{:S(2)}) %collective-permute-start.5) | collective-permute-done | bytes 4194336 | tf_op jit(solution)/shard_map/ppermute | solution.py:18
  638.2 9.3 add_select_fusion.5
  649.7 91.6 %collective-permute-done.6 = f32[2,256,2048]{2,1,0:T(8,128)} collective-permute-done((f32[2,256,2048]{2,1,0:T(8,128)}, f32[2,256,2048]{2,1,0:T(8,128)}, u32[]{:S(2)}, u32[]{:S(2)}) %collective-permute-start.6) | collective-permute-done | bytes 4194336 | tf_op jit(solution)/shard_map/ppermute | solution.py:18
  741.3 86.3 %collective-permute-done.7 = f32[2,256,2048]{2,1,0:T(8,128)} collective-permute-done((f32[2,256,2048]{2,1,0:T(8,128)}, f32[2,256,2048]{2,1,0:T(8,128)}, u32[]{:S(2)}, u32[]{:S(2)}) %collective-permute-start.7) | collective-permute-done | bytes 4194336 | tf_op jit(solution)/shard_map/ppermute | solution.py:18
  827.6 9.2 add_select_fusion.3
  836.8 2.7 collective-permute-start.8
  840.5 91.7 %collective-permute-done.8 = f32[2,256,2048]{2,1,0:T(8,128)} collective-permute-done((f32[2,256,2048]{2,1,0:T(8,128)}, f32[2,256,2048]{2,1,0:T(8,128)}, u32[]{:S(2)}, u32[]{:S(2)}) %collective-permute-start.8) | collective-permute-done | bytes 4194336 | tf_op jit(solution)/shard_map/ppermute | solution.py:18
  932.2 85.3 %collective-permute-done.9 = f32[2,256,2048]{2,1,0:T(8,128)} collective-permute-done((f32[2,256,2048]{2,1,0:T(8,128)}, f32[2,256,2048]{2,1,0:T(8,128)}, u32[]{:S(2)}, u32[]{:S(2)}) %collective-permute-start.9) | collective-permute-done | bytes 4194336 | tf_op jit(solution)/shard_map/ppermute | solution.py:18
  1017.5 7.0 add_select_fusion.1
  1024.5 8.2 fusion.2
  1032.8 8.6 fusion.1
  1041.5 8.3 subtract_bitcast_fusion
  1049.8 8.5 add_bitcast_fusion
  1058.8 3.0 fusion.23
  1061.8 3.2 fusion.25
  1065.0 3.0 convolution_add_fusion
  1068.1 3.5 add_bitcast_fusion.1
  1071.6 2.7 collective-permute-start.10
  1075.2 46.5 %collective-permute-done.10 = f32[2,256,1024]{2,1,0:T(8,128)S(1)} collective-permute-done((f32[2,256,1024]{2,1,0:T(8,128)S(1)}, f32[2,256,1024]{2,1,0:T(8,128)S(1)}, u32[]{:S(2)}, u32[]{:S(2)}) %collective-permute-start.10) | collective-permute-done | bytes 2097184 | tf_op jit(solution)/shard_map/ppermute | solution.py:18
  1121.7 39.5 %collective-permute-done.11 = f32[2,256,1024]{2,1,0:T(8,128)S(1)} collective-permute-done((f32[2,256,1024]{2,1,0:T(8,128)S(1)}, f32[2,256,1024]{2,1,0:T(8,128)S(1)}, u32[]{:S(2)}, u32[]{:S(2)}) %collective-permute-start.11) | collective-permute-done | bytes 2097184 | tf_op jit(solution)/shard_map/ppermute | solution.py:18
  1162.7 1.6 collective-permute-start.12
  1165.1 46.3 %collective-permute-done.12 = f32[2,256,1024]{2,1,0:T(8,128)S(1)} collective-permute-done((f32[2,256,1024]{2,1,0:T(8,128)S(1)}, f32[2,256,1024]{2,1,0:T(8,128)S(1)}, u32[]{:S(2)}, u32[]{:S(2)}) %collective-permute-start.12) | collective-permute-done | bytes 2097184 | tf_op jit(solution)/shard_map/ppermute | solution.py:18
  1211.4 38.9 %collective-permute-done.13 = f32[2,256,1024]{2,1,0:T(8,128)S(1)} collective-permute-done((f32[2,256,1024]{2,1,0:T(8,128)S(1)}, f32[2,256,1024]{2,1,0:T(8,128)S(1)}, u32[]{:S(2)}, u32[]{:S(2)}) %collective-permute-start.13) | collective-permute-done | bytes 2097184 | tf_op jit(solution)/shard_map/ppermute | solution.py:18
  1250.2 1.6 add_select_fusion.15
  1251.8 4.4 collective-permute-start.14
  1256.3 46.5 %collective-permute-done.14 = f32[2,256,1024]{2,1,0:T(8,128)S(1)} collective-permute-done((f32[2,256,1024]{2,1,0:T(8,128)S(1)}, f32[2,256,1024]{2,1,0:T(8,128)S(1)}, u32[]{:S(2)}, u32[]{:S(2)}) %collective-permute-start.14) | collective-permute-done | bytes 2097184 | tf_op jit(solution)/shard_map/ppermute | solution.py:18
  1302.7 39.4 %collective-permute-done.15 = f32[2,256,1024]{2,1,0:T(8,128)S(1)} collective-permute-done((f32[2,256,1024]{2,1,0:T(8,128)S(1)}, f32[2,256,1024]{2,1,0:T(8,128)S(1)}, u32[]{:S(2)}, u32[]{:S(2)}) %collective-permute-start.15) | collective-permute-done | bytes 2097184 | tf_op jit(solution)/shard_map/ppermute | solution.py:18
  1342.1 1.6 add_select_fusion.13
  1343.7 1.8 collective-permute-start.16
  1345.8 46.5 %collective-permute-done.16 = f32[2,256,1024]{2,1,0:T(8,128)S(1)} collective-permute-done((f32[2,256,1024]{2,1,0:T(8,128)S(1)}, f32[2,256,1024]{2,1,0:T(8,128)S(1)}, u32[]{:S(2)}, u32[]{:S(2)}) %collective-permute-start.16) | collective-permute-done | bytes 2097184 | tf_op jit(solution)/shard_map/ppermute | solution.py:18
  1392.3 38.9 %collective-permute-done.17 = f32[2,256,1024]{2,1,0:T(8,128)S(1)} collective-permute-done((f32[2,256,1024]{2,1,0:T(8,128)S(1)}, f32[2,256,1024]{2,1,0:T(8,128)S(1)}, u32[]{:S(2)}, u32[]{:S(2)}) %collective-permute-start.17) | collective-permute-done | bytes 2097184 | tf_op jit(solution)/shard_map/ppermute | solution.py:18
  1432.8 4.3 collective-permute-start.18
  1437.2 46.4 %collective-permute-done.18 = f32[2,256,1024]{2,1,0:T(8,128)S(1)} collective-permute-done((f32[2,256,1024]{2,1,0:T(8,128)S(1)}, f32[2,256,1024]{2,1,0:T(8,128)S(1)}, u32[]{:S(2)}, u32[]{:S(2)}) %collective-permute-start.18) | collective-permute-done | bytes 2097184 | tf_op jit(solution)/shard_map/ppermute | solution.py:18
  1483.7 39.3 %collective-permute-done.19 = f32[2,256,1024]{2,1,0:T(8,128)S(1)} collective-permute-done((f32[2,256,1024]{2,1,0:T(8,128)S(1)}, f32[2,256,1024]{2,1,0:T(8,128)S(1)}, u32[]{:S(2)}, u32[]{:S(2)}) %collective-permute-start.19) | collective-permute-done | bytes 2097184 | tf_op jit(solution)/shard_map/ppermute | solution.py:18
  1524.0 1.8 fusion.12
  (45 shorter events, 18.1 us)
Async XLA Ops:
  6.5 1.2 copy-start
  6.5 59.3 %reduce-scatter.2.cloned.1.call-start = ((), (), s32[]{:S(2)}) async-start(), calls=%async_computation.1 | async-start | bytes 5242880 | tf_op jit(solution)/shard_map/reduce_scatter | solution.py:113
  17.9 48.0 %copy-start.8 = (bf16[256,1024]{1,0:T(8,128)(2,1)S(1)}, bf16[256,1024]{1,0:T(8,128)(2,1)}, u32[]{:S(2)}) copy-start(bf16[256,1024]{1,0:T(8,128)(2,1)} %param.9) | copy-start | bytes 1572868
  17.9 49.4 %copy-start.6 = (f32[256,1024]{1,0:T(8,128)S(1)}, f32[256,1024]{1,0:T(8,128)}, u32[]{:S(2)}) copy-start(f32[256,1024]{1,0:T(8,128)} %param.10) | copy-start | bytes 3145732
  67.3 1.0 copy-start.4
  67.3 2.0 copy-start.7
  67.5 2.3 copy-start.2
  69.8 2.7 copy-start.3
  72.5 95.2 %collective-permute-start = (f32[2,256,2048]{2,1,0:T(8,128)}, f32[2,256,2048]{2,1,0:T(8,128)}, u32[]{:S(2)}, u32[]{:S(2)}) collective-permute-start(f32[2,256,2048]{2,1,0:T(8,128)} %pad_maximum_fusion), channel_id=1, source_target_pairs={{0,64},{64,0},{4,68},{68,4},{8,72},{72,8},{12,76},{76,12},{16,80},... | collective-permute-start | bytes 12582920 | tf_op jit(solution)/shard_map/ppermute | solution.py:18
  78.0 178.8 %collective-permute-start.1 = (f32[2,256,2048]{2,1,0:T(8,128)}, f32[2,256,2048]{2,1,0:T(8,128)}, u32[]{:S(2)}, u32[]{:S(2)}) collective-permute-start(f32[2,256,2048]{2,1,0:T(8,128)} %stack.13), channel_id=1, source_target_pairs={{0,64},{64,0},{4,68},{68,4},{8,72},{72,8},{12,76},{76,12},{16,80},... | collective-permute-start | bytes 12582920 | tf_op jit(solution)/shard_map/ppermute | solution.py:18
  264.6 93.8 %collective-permute-start.2 = (f32[2,256,2048]{2,1,0:T(8,128)}, f32[2,256,2048]{2,1,0:T(8,128)}, u32[]{:S(2)}, u32[]{:S(2)}) collective-permute-start(f32[2,256,2048]{2,1,0:T(8,128)} %get-tuple-element.13), channel_id=1, source_target_pairs={{0,32},{32,0},{4,36},{36,4},{8,40},{40,8},{12,44},{44,12},{16,48},... | collective-permute-start | bytes 12582920 | tf_op jit(solution)/shard_map/ppermute | solution.py:18
  266.0 180.5 %collective-permute-start.3 = (f32[2,256,2048]{2,1,0:T(8,128)}, f32[2,256,2048]{2,1,0:T(8,128)}, u32[]{:S(2)}, u32[]{:S(2)}) collective-permute-start(f32[2,256,2048]{2,1,0:T(8,128)} %get-tuple-element.14), channel_id=1, source_target_pairs={{0,32},{32,0},{4,36},{36,4},{8,40},{40,8},{12,44},{44,12},{16,48},... | collective-permute-start | bytes 12582920 | tf_op jit(solution)/shard_map/ppermute | solution.py:18
  455.7 95.3 %collective-permute-start.4 = (f32[2,256,2048]{2,1,0:T(8,128)}, f32[2,256,2048]{2,1,0:T(8,128)}, u32[]{:S(2)}, u32[]{:S(2)}) collective-permute-start(f32[2,256,2048]{2,1,0:T(8,128)} %get-tuple-element.11), channel_id=1, source_target_pairs={{0,16},{16,0},{4,20},{20,4},{8,24},{24,8},{12,28},{28,12},{32,48},... | collective-permute-start | bytes 12582920 | tf_op jit(solution)/shard_map/ppermute | solution.py:18
  458.8 179.4 %collective-permute-start.5 = (f32[2,256,2048]{2,1,0:T(8,128)}, f32[2,256,2048]{2,1,0:T(8,128)}, u32[]{:S(2)}, u32[]{:S(2)}) collective-permute-start(f32[2,256,2048]{2,1,0:T(8,128)} %get-tuple-element.12), channel_id=1, source_target_pairs={{0,16},{16,0},{4,20},{20,4},{8,24},{24,8},{12,28},{28,12},{32,48},... | collective-permute-start | bytes 12582920 | tf_op jit(solution)/shard_map/ppermute | solution.py:18
  647.5 93.8 %collective-permute-start.6 = (f32[2,256,2048]{2,1,0:T(8,128)}, f32[2,256,2048]{2,1,0:T(8,128)}, u32[]{:S(2)}, u32[]{:S(2)}) collective-permute-start(f32[2,256,2048]{2,1,0:T(8,128)} %get-tuple-element.9), channel_id=1, source_target_pairs={{0,8},{8,0},{4,12},{12,4},{16,24},{24,16},{20,28},{28,20},{32,40},... | collective-permute-start | bytes 12582920 | tf_op jit(solution)/shard_map/ppermute | solution.py:18
  649.0 178.6 %collective-permute-start.7 = (f32[2,256,2048]{2,1,0:T(8,128)}, f32[2,256,2048]{2,1,0:T(8,128)}, u32[]{:S(2)}, u32[]{:S(2)}) collective-permute-start(f32[2,256,2048]{2,1,0:T(8,128)} %get-tuple-element.10), channel_id=1, source_target_pairs={{0,8},{8,0},{4,12},{12,4},{16,24},{24,16},{20,28},{28,20},{32,40},... | collective-permute-start | bytes 12582920 | tf_op jit(solution)/shard_map/ppermute | solution.py:18
  836.8 95.3 %collective-permute-start.8 = (f32[2,256,2048]{2,1,0:T(8,128)}, f32[2,256,2048]{2,1,0:T(8,128)}, u32[]{:S(2)}, u32[]{:S(2)}) collective-permute-start(f32[2,256,2048]{2,1,0:T(8,128)} %get-tuple-element.7), channel_id=1, source_target_pairs={{0,4},{4,0},{8,12},{12,8},{16,20},{20,16},{24,28},{28,24},{32,36},... | collective-permute-start | bytes 12582920 | tf_op jit(solution)/shard_map/ppermute | solution.py:18
  839.5 178.0 %collective-permute-start.9 = (f32[2,256,2048]{2,1,0:T(8,128)}, f32[2,256,2048]{2,1,0:T(8,128)}, u32[]{:S(2)}, u32[]{:S(2)}) collective-permute-start(f32[2,256,2048]{2,1,0:T(8,128)} %get-tuple-element.8), channel_id=1, source_target_pairs={{0,4},{4,0},{8,12},{12,8},{16,20},{20,16},{24,28},{28,24},{32,36},... | collective-permute-start | bytes 12582920 | tf_op jit(solution)/shard_map/ppermute | solution.py:18
  1071.6 50.2 %collective-permute-start.10 = (f32[2,256,1024]{2,1,0:T(8,128)S(1)}, f32[2,256,1024]{2,1,0:T(8,128)S(1)}, u32[]{:S(2)}, u32[]{:S(2)}) collective-permute-start(f32[2,256,1024]{2,1,0:T(8,128)S(1)} %get-tuple-element.26), channel_id=1, source_target_pairs={{0,4},{4,0},{8,12},{12,8},{16,20},{20,16},{24,28},{28,24},{32,36},... | collective-permute-start | bytes 6291464 | tf_op jit(solution)/shard_map/ppermute | solution.py:18
  1074.3 86.9 %collective-permute-start.11 = (f32[2,256,1024]{2,1,0:T(8,128)S(1)}, f32[2,256,1024]{2,1,0:T(8,128)S(1)}, u32[]{:S(2)}, u32[]{:S(2)}) collective-permute-start(f32[2,256,1024]{2,1,0:T(8,128)S(1)} %get-tuple-element.25), channel_id=1, source_target_pairs={{0,4},{4,0},{8,12},{12,8},{16,20},{20,16},{24,28},{28,24},{32,36},... | collective-permute-start | bytes 6291464 | tf_op jit(solution)/shard_map/ppermute | solution.py:18
  1162.7 48.6 %collective-permute-start.12 = (f32[2,256,1024]{2,1,0:T(8,128)S(1)}, f32[2,256,1024]{2,1,0:T(8,128)S(1)}, u32[]{:S(2)}, u32[]{:S(2)}) collective-permute-start(f32[2,256,1024]{2,1,0:T(8,128)S(1)} %get-tuple-element.22), channel_id=1, source_target_pairs={{0,8},{8,0},{4,12},{12,4},{16,24},{24,16},{20,28},{28,20},{32,40},... | collective-permute-start | bytes 6291464 | tf_op jit(solution)/shard_map/ppermute | solution.py:18
  1164.3 85.9 %collective-permute-start.13 = (f32[2,256,1024]{2,1,0:T(8,128)S(1)}, f32[2,256,1024]{2,1,0:T(8,128)S(1)}, u32[]{:S(2)}, u32[]{:S(2)}) collective-permute-start(f32[2,256,1024]{2,1,0:T(8,128)S(1)} %get-tuple-element.21), channel_id=1, source_target_pairs={{0,8},{8,0},{4,12},{12,4},{16,24},{24,16},{20,28},{28,20},{32,40},... | collective-permute-start | bytes 6291464 | tf_op jit(solution)/shard_map/ppermute | solution.py:18
  1251.8 50.9 %collective-permute-start.14 = (f32[2,256,1024]{2,1,0:T(8,128)S(1)}, f32[2,256,1024]{2,1,0:T(8,128)S(1)}, u32[]{:S(2)}, u32[]{:S(2)}) collective-permute-start(f32[2,256,1024]{2,1,0:T(8,128)S(1)} %get-tuple-element.20), channel_id=1, source_target_pairs={{0,16},{16,0},{4,20},{20,4},{8,24},{24,8},{12,28},{28,12},{32,48},... | collective-permute-start | bytes 6291464 | tf_op jit(solution)/shard_map/ppermute | solution.py:18
  1256.2 85.9 %collective-permute-start.15 = (f32[2,256,1024]{2,1,0:T(8,128)S(1)}, f32[2,256,1024]{2,1,0:T(8,128)S(1)}, u32[]{:S(2)}, u32[]{:S(2)}) collective-permute-start(f32[2,256,1024]{2,1,0:T(8,128)S(1)} %get-tuple-element.19), channel_id=1, source_target_pairs={{0,16},{16,0},{4,20},{20,4},{8,24},{24,8},{12,28},{28,12},{32,48},... | collective-permute-start | bytes 6291464 | tf_op jit(solution)/shard_map/ppermute | solution.py:18
  1343.7 48.6 %collective-permute-start.16 = (f32[2,256,1024]{2,1,0:T(8,128)S(1)}, f32[2,256,1024]{2,1,0:T(8,128)S(1)}, u32[]{:S(2)}, u32[]{:S(2)}) collective-permute-start(f32[2,256,1024]{2,1,0:T(8,128)S(1)} %get-tuple-element.18), channel_id=1, source_target_pairs={{0,32},{32,0},{4,36},{36,4},{8,40},{40,8},{12,44},{44,12},{16,48},... | collective-permute-start | bytes 6291464 | tf_op jit(solution)/shard_map/ppermute | solution.py:18
  1345.5 85.7 %collective-permute-start.17 = (f32[2,256,1024]{2,1,0:T(8,128)S(1)}, f32[2,256,1024]{2,1,0:T(8,128)S(1)}, u32[]{:S(2)}, u32[]{:S(2)}) collective-permute-start(f32[2,256,1024]{2,1,0:T(8,128)S(1)} %get-tuple-element.17), channel_id=1, source_target_pairs={{0,32},{32,0},{4,36},{36,4},{8,40},{40,8},{12,44},{44,12},{16,48},... | collective-permute-start | bytes 6291464 | tf_op jit(solution)/shard_map/ppermute | solution.py:18
  1432.8 50.9 %collective-permute-start.18 = (f32[2,256,1024]{2,1,0:T(8,128)S(1)}, f32[2,256,1024]{2,1,0:T(8,128)S(1)}, u32[]{:S(2)}, u32[]{:S(2)}) collective-permute-start(f32[2,256,1024]{2,1,0:T(8,128)S(1)} %get-tuple-element.16), channel_id=1, source_target_pairs={{0,64},{64,0},{4,68},{68,4},{8,72},{72,8},{12,76},{76,12},{16,80},... | collective-permute-start | bytes 6291464 | tf_op jit(solution)/shard_map/ppermute | solution.py:18
  1437.1 86.9 %copy-start.5 = (f32[256,1024]{1,0:T(8,128)S(1)}, f32[256,1024]{1,0:T(8,128)}, u32[]{:S(2)}) copy-start(f32[256,1024]{1,0:T(8,128)} %copy-done.4) | copy-start | bytes 3145732
  1437.1 86.9 %copy-start.9 = (bf16[256,1024]{1,0:T(8,128)(2,1)S(1)}, bf16[256,1024]{1,0:T(8,128)(2,1)}, u32[]{:S(2)}) copy-start(bf16[256,1024]{1,0:T(8,128)(2,1)} %param.8) | copy-start | bytes 1572868
  1437.1 86.9 %copy-start.10 = (f32[1024]{0:T(1024)S(1)}, f32[1024]{0:T(1024)}, u32[]{:S(2)}) copy-start(f32[1024]{0:T(1024)} %param.11) | copy-start | bytes 12292
  1437.1 85.8 %collective-permute-start.19 = (f32[2,256,1024]{2,1,0:T(8,128)S(1)}, f32[2,256,1024]{2,1,0:T(8,128)S(1)}, u32[]{:S(2)}, u32[]{:S(2)}) collective-permute-start(f32[2,256,1024]{2,1,0:T(8,128)S(1)} %get-tuple-element.15), channel_id=1, source_target_pairs={{0,64},{64,0},{4,68},{68,4},{8,72},{72,8},{12,76},{76,12},{16,80},... | collective-permute-start | bytes 6291464 | tf_op jit(solution)/shard_map/ppermute | solution.py:18
  1524.0 1.8 copy-start.1
Sparse Core Ops, SparseCore 0:
  18.0 47.8 reduce-scatter.1
where the time goes:
time: 1540 us; the launch traced here: 1530 us
  waiting for transfers between devices  1370 us (89%)
  other arithmetic  56.7 us (4%)
  matrix products  56.5 us (4%)
  starting transfers between devices  31.6 us (2%)
    ppermute x20, waiting for transfers between devices, from_partner(): return lax.ppermute(block, axis, route)  1320 us
    reduce_scatter x1, waiting for transfers between devices, body(): lax.psum_scatter(partial_value, 'proj', scatter_dimension=1, tiled=True)  47.8 us
    dot_general x8, matrix products, apply_table(): return jnp.einsum('kj,ejc->ekc', table, values, precision=HIGHEST)  46.4 us
    select_n x5, other arithmetic, by_pairs(): spec_real = jnp.where(upper_half, rot_real, spec_real + other_real)  42.5 us
    ppermute x20, starting transfers between devices, from_partner(): return lax.ppermute(block, axis, route)  31.6 us
  transfers between devices with their start and end apart: 21, of which 21 were waited for; matrix products, arithmetic and copies ran while one was open for 0% of the time, Pallas kernels for 0%

commit v1 on v0

v1 whole, which is shorter than its diff:
```python
import functools

import jax
import jax.numpy as jnp
import ml_dtypes
import numpy as np
from jax import lax
from jax.experimental import pallas as pl
from jax.experimental.pallas import tpu as pltpu
from jax.sharding import PartitionSpec as P

MESH = pl.DeviceIdType.MESH
F32 = jnp.float32
BF16 = jnp.bfloat16
SUB = 8


def odd_tables(block):
    n = np.arange(block)
    k = np.arange(block)
    angle = np.pi / (2 * block) * ((n[:, None] * (2 * k[None, :] + 1)) % (4 * block))
    forward = np.concatenate([np.cos(angle), -np.sin(angle)], axis=1)
    inverse = forward.T / block

    def split(table):
        high = table.astype(np.float32).astype(ml_dtypes.bfloat16)
        low = (table - high.astype(np.float64)).astype(np.float32).astype(ml_dtypes.bfloat16)
        return high, low

    return split(forward) + split(inverse)


def split_rows(values):
    high = values.astype(BF16)
    low = (values - high.astype(F32)).astype(BF16)
    return high, low


def dot(a, b):
    return jnp.dot(a, b, preferred_element_type=F32)


def table_dot(values, table_high, table_low):
    rows = values.shape[0]
    high, low = split_rows(values)
    both = dot(jnp.concatenate([high, low], axis=0), table_high)
    return both[:rows] + both[rows:] + dot(high, table_low)


def kernel(
    seq_count, chunks,
    tokens_h, weight_h, query_h, keyed_h, filters_h, skip_v, fwd_high_h, fwd_low_h, inv_high_h, inv_low_h,
    out_h,
    tokens_v, weight_v, query_v, keyed_v, filters_v, fwd_high, fwd_low, inv_high, inv_low,
    near_send, near_recv, far_send, far_recv, own_far, own_near, gated_v,
    filt_send, filt_recv, sig_send, sig_recv, back_send, back_recv, out_v,
    filt_spec, sig_spec, prod_spec,
    load_sem, weight_sem, near_send_sem, near_recv_sem, far_send_sem, far_recv_sem,
    filt_send_sem, filt_recv_sem, sig_send_sem, sig_recv_sem, back_send_sem, back_recv_sem, out_sem,
):
    seq = lax.axis_index("seq")
    proj = lax.axis_index("proj")
    core = lax.rem(proj, 2)
    side = proj // 2
    core_partner = side * 2 + 1 - core
    chip_partner = (1 - side) * 2 + core
    rows = tokens_h.shape[0]
    width = skip_v.shape[1]
    step = width // chunks
    blocks = seq_count // 2
    block = 2 * rows

    def columns(start):
        return pl.ds(pl.multiple_of(start, step), step)

    filter_load = pltpu.make_async_copy(filters_h, filters_v, load_sem.at[0])
    token_load = pltpu.make_async_copy(tokens_h, tokens_v, load_sem.at[1])
    filter_load.start()
    token_load.start()
    quarters = ((1 - side) * 2 + 1 - core, (1 - side) * 2 + core, side * 2 + 1 - core, side * 2 + core)

    def weight_load(quarter, n):
        slot = quarter * chunks + n
        return pltpu.make_async_copy(
            weight_h.at[:, columns(quarters[quarter] * width + n * step)], weight_v.at[slot], weight_sem.at[slot]
        )

    for pair in range(2):
        for n in range(chunks):
            weight_load(2 * pair, n).start()
            weight_load(2 * pair + 1, n).start()
    table_loads = [
        pltpu.make_async_copy(src, dst, load_sem.at[2 + i])
        for i, (src, dst) in enumerate(
            ((fwd_high_h, fwd_high), (fwd_low_h, fwd_low), (inv_high_h, inv_high), (inv_low_h, inv_low))
        )
    ]
    for copy in table_loads:
        copy.start()
    part_loads = []
    for n in range(chunks):
        part_loads.append(pltpu.make_async_copy(keyed_h.at[:, pl.ds(n * step, step)], keyed_v.at[n], load_sem.at[6 + n]))
        part_loads.append(
            pltpu.make_async_copy(query_h.at[:, pl.ds(n * step, step)], query_v.at[n], load_sem.at[6 + chunks + n])
        )
    for copy in part_loads:
        copy.start()

    barrier = pltpu.get_barrier_semaphore()

    def greet(d, carry):
        peer = lax.rem(seq + d, seq_count)
        pl.semaphore_signal(barrier, inc=1, device_id=(peer, proj), device_id_type=MESH)
        return carry

    lax.fori_loop(1, seq_count, greet, 0)
    for partner in (core_partner, chip_partner):
        pl.semaphore_signal(barrier, inc=1, device_id=(seq, partner), device_id_type=MESH)
    pl.semaphore_wait(barrier, seq_count + 1)

    def spread(source, target, send_sem, recv_sem):
        def send(d, carry):
            peer = lax.rem(seq + d, seq_count)
            pltpu.make_async_remote_copy(
                src_ref=source(peer), dst_ref=target(seq), send_sem=send_sem, recv_sem=recv_sem,
                device_id=(peer, proj), device_id_type=MESH,
            ).start()
            return carry

        pltpu.make_async_copy(source(seq), target(seq), recv_sem).start()
        lax.fori_loop(1, seq_count, send, 0)

    def await_bytes(ref, sem):
        pltpu.make_async_copy(ref, ref, sem).wait()

    filter_load.wait()

    def send_filters(n, carry):
        part = filters_v[:, columns(n * step)].T
        filt_send[:, pl.ds(n, 1)] = part.reshape(seq_count, 1, SUB, rows)
        return carry

    lax.fori_loop(0, chunks, send_filters, 0)
    spread(lambda r: filt_send.at[r], lambda r: filt_recv.at[r], filt_send_sem, filt_recv_sem)

    token_load.wait()

    def project(quarter, n):
        weight_load(quarter, n).wait()
        return dot(tokens_v[...], weight_v[quarter * chunks + n])

    def near_copy(pair, n):
        return pltpu.make_async_remote_copy(
            src_ref=near_send.at[pair, n], dst_ref=near_recv.at[pair, n],
            send_sem=near_send_sem.at[pair, n], recv_sem=near_recv_sem.at[pair, n],
            device_id=(seq, core_partner), device_id_type=MESH,
        )

    def far_copy(n):
        return pltpu.make_async_remote_copy(
            src_ref=far_send.at[n], dst_ref=far_recv.at[n],
            send_sem=far_send_sem.at[n], recv_sem=far_recv_sem.at[n],
            device_id=(seq, chip_partner), device_id_type=MESH,
        )

    def send_far(n):
        near_copy(0, n).wait_recv()
        far_send[n] = own_far[n] + near_recv[0, n]
        far_copy(n).start()

    def project_far(n, carry):
        near_send[0, n] = project(0, n)
        near_copy(0, n).start()
        own_far[n] = project(1, n)

        @pl.when(n > 0)
        def _():
            send_far(n - 1)

        return carry

    lax.fori_loop(0, chunks, project_far, 0)
    send_far(chunks - 1)

    def project_near(n, carry):
        near_send[1, n] = project(2, n)
        near_copy(1, n).start()
        own_near[n] = project(3, n)
        return carry

    lax.fori_loop(0, chunks, project_near, 0)

    for copy in table_loads:
        copy.wait()
    await_bytes(filt_recv, filt_recv_sem)
    flip = (1 - 2 * lax.rem(lax.broadcasted_iota(jnp.int32, (1, 1, block), 2), 2)).astype(F32)

    def block_spectra(values):
        pairs = values.reshape(blocks, 2, SUB, rows)
        joined = jnp.concatenate([pairs[:, 0], pairs[:, 1]], axis=2).reshape(blocks * SUB, block)
        return table_dot(joined, fwd_high[...], fwd_low[...]).reshape(blocks, SUB, 2 * block)

    def filter_spectra(n, carry):
        spec = block_spectra(filt_recv[:, pl.ds(n, 1)].reshape(seq_count, SUB, rows))
        filt_spec[n] = spec
        filt_spec[n, 1:, :, :block] = spec[1:, :, :block] - flip * spec[:-1, :, block:]
        filt_spec[n, 1:, :, block:] = spec[1:, :, block:] + flip * spec[:-1, :, :block]
        return carry

    lax.fori_loop(0, chunks, filter_spectra, 0)
    for copy in part_loads:
        copy.wait()

    def gate(n):
        near_copy(1, n).wait_recv()
        far_copy(n).wait_recv()
        valued = own_near[n] + near_recv[1, n] + far_recv[n]
        gated = keyed_v[n].astype(F32) * valued
        gated_v[n] = gated
        sig_send[n] = gated.T.reshape(seq_count, SUB, rows)
        spread(
            lambda r: sig_send.at[n, r], lambda r: sig_recv.at[n, r], sig_send_sem.at[n], sig_recv_sem.at[n]
        )

    def convolve(n):
        await_bytes(sig_recv.at[n], sig_recv_sem.at[n])
        sig_spec[...] = block_spectra(sig_recv[n])

        def lanes(part, carry):
            re = pl.ds(pl.multiple_of(part * 128, 128), 128)
            im = pl.ds(pl.multiple_of(block + part * 128, 128), 128)
            sig_re = [sig_spec[j, :, re] for j in range(blocks)]
            sig_im = [sig_spec[j, :, im] for j in range(blocks)]
            for s in range(blocks):
                sum_re = sum_im = None
                for j in range(s + 1):
                    tap_re, tap_im = filt_spec[n, j, :, re], filt_spec[n, j, :, im]
                    x_re, x_im = sig_re[s - j], sig_im[s - j]
                    term_re = tap_re * x_re - tap_im * x_im
                    term_im = tap_re * x_im + tap_im * x_re
                    sum_re = term_re if sum_re is None else sum_re + term_re
                    sum_im = term_im if sum_im is None else sum_im + term_im
                prod_spec[s, :, re] = sum_re
                prod_spec[s, :, im] = sum_im
            return carry

        lax.fori_loop(0, block // 128, lanes, 0)
        result = table_dot(
            prod_spec[...].reshape(blocks * SUB, 2 * block), inv_high[...], inv_low[...]
        ).reshape(blocks, SUB, block)
        pairs = jnp.stack([result[:, :, :rows], result[:, :, rows:]], axis=1)
        back_send[n] = pairs.reshape(seq_count, SUB, rows)
        spread(
            lambda r: back_send.at[n, r], lambda r: back_recv.at[n, r], back_send_sem.at[n], back_recv_sem.at[n]
        )

    def out_copy(n):
        return pltpu.make_async_copy(out_v.at[n], out_h.at[:, columns(n * step)], out_sem.at[n])

    def finish(n):
        await_bytes(back_recv.at[n], back_recv_sem.at[n])
        conv = back_recv[n].reshape(step, rows).T
        skip = skip_v[:, columns(n * step)]
        out_v[n] = (query_v[n].astype(F32) * (conv + skip * gated_v[n])).astype(BF16)
        out_copy(n).start()

    def stage(i, carry):
        @pl.when(i < chunks)
        def _():
            gate(i)

        @pl.when(jnp.logical_and(i >= 1, i <= chunks))
        def _():
            convolve(i - 1)

        @pl.when(i >= 2)
        def _():
            finish(i - 2)

        return carry

    lax.fori_loop(0, chunks + 2, stage, 0)

    def drain(n, carry):
        near_copy(0, n).wait_send()
        near_copy(1, n).wait_send()
        far_copy(n).wait_send()
        await_bytes(sig_send.at[n, pl.ds(0, seq_count - 1)], sig_send_sem.at[n])
        await_bytes(back_send.at[n, pl.ds(0, seq_count - 1)], back_send_sem.at[n])
        out_copy(n).wait()
        return carry

    await_bytes(filt_send.at[pl.ds(0, seq_count - 1)], filt_send_sem)
    lax.fori_loop(0, chunks, drain, 0)


def body(seq_count, tokens, value_weight, query, keyed, filters, skip_gain):
    rows, depth = tokens.shape
    width = skip_gain.shape[0]
    chunks = width // (seq_count * SUB)
    step = width // chunks
    block = 2 * rows
    blocks = seq_count // 2
    tables = [jnp.asarray(table) for table in odd_tables(block)]
    any_space = pl.BlockSpec(memory_space=pl.ANY)
    dma = pltpu.SemaphoreType.DMA
    strip = pltpu.VMEM((chunks, rows, step), F32)
    pieces = pltpu.VMEM((chunks, seq_count, SUB, rows), F32)
    filt_pieces = pltpu.VMEM((seq_count, chunks, SUB, rows), F32)
    return pl.pallas_call(
        functools.partial(kernel, seq_count, chunks),
        out_shape=jax.ShapeDtypeStruct((rows, width), BF16),
        in_specs=[any_space] * 5 + [pl.BlockSpec(memory_space=pltpu.VMEM)] + [any_space] * 4,
        out_specs=any_space,
        scratch_shapes=[
            pltpu.VMEM((rows, depth), BF16),
            pltpu.VMEM((4 * chunks, depth, step), BF16),
            pltpu.VMEM((chunks, rows, step), BF16),
            pltpu.VMEM((chunks, rows, step), BF16),
            pltpu.VMEM((rows, width), F32),
            pltpu.VMEM((block, 2 * block), BF16),
            pltpu.VMEM((block, 2 * block), BF16),
            pltpu.VMEM((2 * block, block), BF16),
            pltpu.VMEM((2 * block, block), BF16),
            pltpu.VMEM((2, chunks, rows, step), F32),
            pltpu.VMEM((2, chunks, rows, step), F32),
            strip, strip, strip, strip, strip,
            filt_pieces, filt_pieces, pieces, pieces, pieces, pieces,
            pltpu.VMEM((chunks, rows, step), BF16),
            pltpu.VMEM((chunks, blocks, SUB, 2 * block), F32),
            pltpu.VMEM((blocks, SUB, 2 * block), F32),
            pltpu.VMEM((blocks, SUB, 2 * block), F32),
            dma((6 + 2 * chunks,)), dma((4 * chunks,)),
            dma((2, chunks)), dma((2, chunks)), dma((chunks,)), dma((chunks,)),
            dma, dma, dma((chunks,)), dma((chunks,)), dma((chunks,)), dma((chunks,)), dma((chunks,)),
        ],
        compiler_params=pltpu.CompilerParams(
            collective_id=0, has_side_effects=True, vmem_limit_bytes=56 * 1024 * 1024
        ),
    )(tokens, value_weight, query, keyed, filters, skip_gain.reshape(1, width), *tables)


def solution(mesh):
    in_specs = (
        P("seq", "proj"),
        P("proj", None),
        P("seq", "proj"),
        P("seq", "proj"),
        P("seq", "proj"),
        P("proj"),
    )
    return jax.shard_map(
        functools.partial(body, mesh.shape["seq"]), mesh=mesh, in_specs=in_specs, out_specs=P("seq", "proj"), check_vma=False
    )
```

time: 1540 us -> 82.4 us (0.05)
  waiting for transfers between devices: 1370 us -> 0 us
  Pallas kernels: 0 us -> 80.4 us
  other arithmetic: 56.7 us -> 0 us
  matrix products: 56.5 us -> 0 us
  starting transfers between devices: 31.6 us -> 0 us
    ppermute x20 -> x0, waiting for transfers between devices: 1320 us -> none  [from_partner(): return lax.ppermute(block, axis, route)]
    pallas_call x0 -> x1, Pallas kernels: none -> 80.4 us  [body(): pl.pallas_call(functools.partial(kernel, seq_count, chunks), out_shape=ja...]
    dot_general x9 -> x0, matrix products: 56.5 us -> none  [the longest x8 46.4 us: apply_table(): return jnp.einsum('kj,ejc->ekc', table, values, precision=HIGHEST)]
    select_n x10 -> x0, other arithmetic: 49.8 us -> none  [the longest x5 42.5 us: by_pairs(): spec_real = jnp.where(upper_half, rot_real, spec_real + other_real)]
    reduce_scatter x1 -> x0, waiting for transfers between devices: 47.8 us -> none  [body(): lax.psum_scatter(partial_value, 'proj', scatter_dimension=1, tiled=True)]
    ppermute x20 -> x0, starting transfers between devices: 31.6 us -> none  [from_partner(): return lax.ppermute(block, axis, route)]
  transfers between devices with their start and end apart: 21 -> 0, of which waited for: 21 -> 0; matrix products, arithmetic and copies ran while one was open for 0% -> 0% of each run, Pallas kernels for 0% -> 0%
where the time goes in v1:
time: 82.4 us; the launch traced here: 82.3 us
  Pallas kernels  80.4 us (98%)
  local copies, waits for them, and re-layouts  1.87 us (2%)
    pallas_call x1, Pallas kernels, body(): pl.pallas_call(functools.partial(kernel, seq_count, chunks), out_shape=ja...  80.4 us
    unnamed x1, local copies, waits for them, and re-layouts  1.87 us

profile of v1, /device:TPU:0, one launch (start us, length us, event | category | flops | bytes accessed | tf_op | source)
XLA Modules:
  0.0 82.3 jit_solution(3989388072295799002)
XLA Ops:
  0.0 80.4 %shard_map.100 = bf16[256,1024]{1,0:T(8,128)(2,1)} custom-call(bf16[256,2048]{1,0:T(8,128)(2,1)} %tokens_h.1, bf16[2048,4096]{1,0:T(8,128)(2,1)} %weight_h.1, bf16[256,1024]{1,0:T(8,128)(2,1)} %query_h.1, bf16[256,1024]{1,0:T(8,128)(2,1)} %keyed_h.1, f32[256,1024]{1,0:T(8,128)} %filters_h.1, f32[1,1024]{1,0:T(1,128)} %bitcast.1, ...), custom_call_target="tpu_custom_call" | custom-call | tf_op jit(solution)/shard_map/pallas_call | solution.py:310
  80.4 1.9 %copy.12 = bf16[256,1024]{1,0:T(8,128)(2,1)} copy(bf16[256,1024]{1,0:T(8,128)(2,1)} %shard_map.100) | data formatting | bytes 1048576

commit v2 on v1

--- a/solution.py
+++ b/solution.py
@@ -1,4 +1,5 @@
 import functools
+import math
 
 import jax
 import jax.numpy as jnp
@@ -13,6 +14,7 @@
 F32 = jnp.float32
 BF16 = jnp.bfloat16
 SUB = 8
+LAG = 4
 
 
 def odd_tables(block):
@@ -48,7 +50,7 @@
 
 
 def kernel(
-    seq_count, chunks,
+    edge, seq_count, chunks,
     tokens_h, weight_h, query_h, keyed_h, filters_h, skip_v, fwd_high_h, fwd_low_h, inv_high_h, inv_low_h,
     out_h,
     tokens_v, weight_v, query_v, keyed_v, filters_v, fwd_high, fwd_low, inv_high, inv_low,
@@ -56,7 +58,7 @@
     filt_send, filt_recv, sig_send, sig_recv, back_send, back_recv, out_v,
     filt_spec, sig_spec, prod_spec,
     load_sem, weight_sem, near_send_sem, near_recv_sem, far_send_sem, far_recv_sem,
-    filt_send_sem, filt_recv_sem, sig_send_sem, sig_recv_sem, back_send_sem, back_recv_sem, out_sem,
+    filt_send_sem, filt_recv_sem, sig_send_sem, sig_recv_sem, back_send_sem, back_recv_sem, out_sem, round_sem,
 ):
     seq = lax.axis_index("seq")
     proj = lax.axis_index("proj")
@@ -106,21 +108,28 @@
     for copy in part_loads:
         copy.start()
 
+    row, column, half = seq // (2 * edge), lax.rem(seq // 2, edge), lax.rem(seq, 2)
+
+    def place(d):
+        return (
+            lax.rem(row + d // (2 * edge), edge) * edge + lax.rem(column + lax.rem(d // 2, edge), edge)
+        ) * 2 + lax.rem(half + lax.rem(d, 2), 2)
+
     barrier = pltpu.get_barrier_semaphore()
 
-    def greet(d, carry):
-        peer = lax.rem(seq + d, seq_count)
-        pl.semaphore_signal(barrier, inc=1, device_id=(peer, proj), device_id_type=MESH)
-        return carry
-
-    lax.fori_loop(1, seq_count, greet, 0)
-    for partner in (core_partner, chip_partner):
-        pl.semaphore_signal(barrier, inc=1, device_id=(seq, partner), device_id_type=MESH)
-    pl.semaphore_wait(barrier, seq_count + 1)
+    def greet(sem, peer, part):
+        pl.semaphore_signal(sem, inc=1, device_id=(peer, part), device_id_type=MESH)
+
+    for d in range(1, edge):
+        greet(barrier, place(2 * d), proj)
+        greet(barrier, place(2 * edge * d), proj)
+    greet(barrier, place(1), proj)
+    greet(barrier, seq, core_partner)
+    greet(barrier, seq, chip_partner)
 
     def spread(source, target, send_sem, recv_sem):
         def send(d, carry):
-            peer = lax.rem(seq + d, seq_count)
+            peer = place(d)
             pltpu.make_async_remote_copy(
                 src_ref=source(peer), dst_ref=target(seq), send_sem=send_sem, recv_sem=recv_sem,
                 device_id=(peer, proj), device_id_type=MESH,
@@ -133,16 +142,6 @@
     def await_bytes(ref, sem):
         pltpu.make_async_copy(ref, ref, sem).wait()
 
-    filter_load.wait()
-
-    def send_filters(n, carry):
-        part = filters_v[:, columns(n * step)].T
-        filt_send[:, pl.ds(n, 1)] = part.reshape(seq_count, 1, SUB, rows)
-        return carry
-
-    lax.fori_loop(0, chunks, send_filters, 0)
-    spread(lambda r: filt_send.at[r], lambda r: filt_recv.at[r], filt_send_sem, filt_recv_sem)
-
     token_load.wait()
 
     def project(quarter, n):
@@ -168,18 +167,42 @@
         far_send[n] = own_far[n] + near_recv[0, n]
         far_copy(n).start()
 
-    def project_far(n, carry):
+    def project_far(n):
         near_send[0, n] = project(0, n)
         near_copy(0, n).start()
         own_far[n] = project(1, n)
 
-        @pl.when(n > 0)
-        def _():
-            send_far(n - 1)
-
-        return carry
-
-    lax.fori_loop(0, chunks, project_far, 0)
+    near_send[0, 0] = project(0, 0)
+    own_far[0] = project(1, 0)
+    pl.semaphore_wait(barrier, 2 * edge + 1)
+    near_copy(0, 0).start()
+    for d in range(1, edge):
+        greet(round_sem.at[0], place(2 * d), proj)
+    project_far(1)
+    pl.semaphore_wait(round_sem.at[0], edge - 1)
+    greet(round_sem.at[1], place(1), proj)
+    send_far(0)
+    project_far(2)
+    send_far(1)
+    pl.semaphore_wait(round_sem.at[1], 1)
+
+    filter_load.wait()
+
+    def send_filters(n, carry):
+        part = filters_v[:, columns(n * step)].T
+        filt_send[:, pl.ds(n, 1)] = part.reshape(seq_count, 1, SUB, rows)
+        return carry
+
+    lax.fori_loop(0, chunks, send_filters, 0)
+    spread(lambda r: filt_send.at[r], lambda r: filt_recv.at[r], filt_send_sem, filt_recv_sem)
+
+
+    def project_rest(n, carry):
+        project_far(n)
+        send_far(n - 1)
+        return carry
+
+    lax.fori_loop(3, chunks, project_rest, 0)
     send_far(chunks - 1)
 
     def project_near(n, carry):
@@ -269,17 +292,19 @@
         def _():
             gate(i)
 
-        @pl.when(jnp.logical_and(i >= 1, i <= chunks))
+        @pl.when(i >= LAG)
         def _():
-            convolve(i - 1)
-
-        @pl.when(i >= 2)
-        def _():
-            finish(i - 2)
-
-        return carry
-
-    lax.fori_loop(0, chunks + 2, stage, 0)
+            convolve(i - LAG)
+
+        return carry
+
+    lax.fori_loop(0, chunks + LAG, stage, 0)
+
+    def last(n, carry):
+        finish(n)
+        return carry
+
+    lax.fori_loop(0, chunks, last, 0)
 
     def drain(n, carry):
         near_copy(0, n).wait_send()
@@ -308,7 +333,7 @@
     pieces = pltpu.VMEM((chunks, seq_count, SUB, rows), F32)
     filt_pieces = pltpu.VMEM((seq_count, chunks, SUB, rows), F32)
     return pl.pallas_call(
-        functools.partial(kernel, seq_count, chunks),
+        functools.partial(kernel, math.isqrt(seq_count // 2), seq_count, chunks),
         out_shape=jax.ShapeDtypeStruct((rows, width), BF16),
         in_specs=[any_space] * 5 + [pl.BlockSpec(memory_space=pltpu.VMEM)] + [any_space] * 4,
         out_specs=any_space,
@@ -333,6 +358,7 @@
             dma((6 + 2 * chunks,)), dma((4 * chunks,)),
             dma((2, chunks)), dma((2, chunks)), dma((chunks,)), dma((chunks,)),
             dma, dma, dma((chunks,)), dma((chunks,)), dma((chunks,)), dma((chunks,)), dma((chunks,)),
+            pltpu.SemaphoreType.REGULAR((2,)),
         ],
         compiler_params=pltpu.CompilerParams(
             collective_id=0, has_side_effects=True, vmem_limit_bytes=56 * 1024 * 1024

time: 82.4 us -> 76.3 us (0.926)
  Pallas kernels: 80.4 us -> 74.2 us
    pallas_call x1, Pallas kernels: 80.4 us -> 74.2 us  [body(): pl.pallas_call(functools.partial(kernel, math.isqrt(seq_count // 2), seq_...]
where the time goes in v2:
time: 76.3 us; the launch traced here: 76.1 us
  Pallas kernels  74.2 us (97%)
  local copies, waits for them, and re-layouts  1.87 us (2%)
    pallas_call x1, Pallas kernels, body(): pl.pallas_call(functools.partial(kernel, math.isqrt(seq_count // 2), seq_...  74.2 us
    unnamed x1, local copies, waits for them, and re-layouts  1.87 us

profile of v2, /device:TPU:0, one launch (start us, length us, event | category | flops | bytes accessed | tf_op | source)
XLA Modules:
  0.0 76.1 jit_solution(12033843460062666980)
XLA Ops:
  0.0 74.2 %shard_map.100 = bf16[256,1024]{1,0:T(8,128)(2,1)} custom-call(bf16[256,2048]{1,0:T(8,128)(2,1)} %tokens_h.1, bf16[2048,4096]{1,0:T(8,128)(2,1)} %weight_h.1, bf16[256,1024]{1,0:T(8,128)(2,1)} %query_h.1, bf16[256,1024]{1,0:T(8,128)(2,1)} %keyed_h.1, f32[256,1024]{1,0:T(8,128)} %filters_h.1, f32[1,1024]{1,0:T(1,128)} %bitcast.1, ...), custom_call_target="tpu_custom_call" | custom-call | tf_op jit(solution)/shard_map/pallas_call | solution.py:335
  74.2 1.9 %copy.12 = bf16[256,1024]{1,0:T(8,128)(2,1)} copy(bf16[256,1024]{1,0:T(8,128)(2,1)} %shard_map.100) | data formatting | bytes 1048576

commit v3 on v2

--- a/solution.py
+++ b/solution.py
@@ -14,6 +14,8 @@
 F32 = jnp.float32
 BF16 = jnp.bfloat16
 SUB = 8
+EAGER = True
+SPEC_AT = 0
 LAG = 4
 
 
@@ -54,7 +56,7 @@
     tokens_h, weight_h, query_h, keyed_h, filters_h, skip_v, fwd_high_h, fwd_low_h, inv_high_h, inv_low_h,
     out_h,
     tokens_v, weight_v, query_v, keyed_v, filters_v, fwd_high, fwd_low, inv_high, inv_low,
-    near_send, near_recv, far_send, far_recv, own_far, own_near, gated_v,
+    partial_v, near_recv, far_send, far_recv, gated_v,
     filt_send, filt_recv, sig_send, sig_recv, back_send, back_recv, out_v,
     filt_spec, sig_spec, prod_spec,
     load_sem, weight_sem, near_send_sem, near_recv_sem, far_send_sem, far_recv_sem,
@@ -77,36 +79,29 @@
 
     filter_load = pltpu.make_async_copy(filters_h, filters_v, load_sem.at[0])
     token_load = pltpu.make_async_copy(tokens_h, tokens_v, load_sem.at[1])
-    filter_load.start()
     token_load.start()
-    quarters = ((1 - side) * 2 + 1 - core, (1 - side) * 2 + core, side * 2 + 1 - core, side * 2 + core)
-
-    def weight_load(quarter, n):
-        slot = quarter * chunks + n
-        return pltpu.make_async_copy(
-            weight_h.at[:, columns(quarters[quarter] * width + n * step)], weight_v.at[slot], weight_sem.at[slot]
-        )
-
-    for pair in range(2):
-        for n in range(chunks):
-            weight_load(2 * pair, n).start()
-            weight_load(2 * pair + 1, n).start()
+
+    def weight_load(k):
+        pair, inner = k // (2 * chunks), lax.rem(k, 2 * chunks)
+        home_side = side + (1 - pair) * (1 - 2 * side)
+        home_core = core + (1 - lax.rem(inner, 2)) * (1 - 2 * core)
+        start = (home_side * 2 + home_core) * width + inner // 2 * step
+        return pltpu.make_async_copy(weight_h.at[:, columns(start)], weight_v.at[k], weight_sem.at[k])
+
+    weight_load(0).start()
+    weight_load(1).start()
     table_loads = [
         pltpu.make_async_copy(src, dst, load_sem.at[2 + i])
         for i, (src, dst) in enumerate(
             ((fwd_high_h, fwd_high), (fwd_low_h, fwd_low), (inv_high_h, inv_high), (inv_low_h, inv_low))
         )
     ]
-    for copy in table_loads:
-        copy.start()
     part_loads = []
     for n in range(chunks):
         part_loads.append(pltpu.make_async_copy(keyed_h.at[:, pl.ds(n * step, step)], keyed_v.at[n], load_sem.at[6 + n]))
         part_loads.append(
             pltpu.make_async_copy(query_h.at[:, pl.ds(n * step, step)], query_v.at[n], load_sem.at[6 + chunks + n])
         )
-    for copy in part_loads:
-        copy.start()
 
     row, column, half = seq // (2 * edge), lax.rem(seq // 2, edge), lax.rem(seq, 2)
 
@@ -144,13 +139,9 @@
 
     token_load.wait()
 
-    def project(quarter, n):
-        weight_load(quarter, n).wait()
-        return dot(tokens_v[...], weight_v[quarter * chunks + n])
-
     def near_copy(pair, n):
         return pltpu.make_async_remote_copy(
-            src_ref=near_send.at[pair, n], dst_ref=near_recv.at[pair, n],
+            src_ref=partial_v.at[2 * chunks * pair + 2 * n], dst_ref=near_recv.at[pair, n],
             send_sem=near_send_sem.at[pair, n], recv_sem=near_recv_sem.at[pair, n],
             device_id=(seq, core_partner), device_id_type=MESH,
         )
@@ -162,60 +153,86 @@
             device_id=(seq, chip_partner), device_id_type=MESH,
         )
 
-    def send_far(n):
+    def sum_far(n):
         near_copy(0, n).wait_recv()
-        far_send[n] = own_far[n] + near_recv[0, n]
-        far_copy(n).start()
-
-    def project_far(n):
-        near_send[0, n] = project(0, n)
-        near_copy(0, n).start()
-        own_far[n] = project(1, n)
-
-    near_send[0, 0] = project(0, 0)
-    own_far[0] = project(1, 0)
-    pl.semaphore_wait(barrier, 2 * edge + 1)
-    near_copy(0, 0).start()
-    for d in range(1, edge):
-        greet(round_sem.at[0], place(2 * d), proj)
-    project_far(1)
-    pl.semaphore_wait(round_sem.at[0], edge - 1)
-    greet(round_sem.at[1], place(1), proj)
-    send_far(0)
-    project_far(2)
-    send_far(1)
-    pl.semaphore_wait(round_sem.at[1], 1)
-
-    filter_load.wait()
-
-    def send_filters(n, carry):
+        far_send[n] = partial_v[2 * n + 1] + near_recv[0, n]
+
+    def transpose_filters(n, carry):
         part = filters_v[:, columns(n * step)].T
         filt_send[:, pl.ds(n, 1)] = part.reshape(seq_count, 1, SUB, rows)
         return carry
 
-    lax.fori_loop(0, chunks, send_filters, 0)
-    spread(lambda r: filt_send.at[r], lambda r: filt_recv.at[r], filt_send_sem, filt_recv_sem)
-
-
-    def project_rest(n, carry):
-        project_far(n)
-        send_far(n - 1)
-        return carry
-
-    lax.fori_loop(3, chunks, project_rest, 0)
-    send_far(chunks - 1)
-
-    def project_near(n, carry):
-        near_send[1, n] = project(2, n)
-        near_copy(1, n).start()
-        own_near[n] = project(3, n)
-        return carry
-
-    lax.fori_loop(0, chunks, project_near, 0)
-
-    for copy in table_loads:
+    def project(k, carry):
+        weight_load(k).wait()
+
+        @pl.when(k + 2 < 4 * chunks)
+        def _():
+            weight_load(k + 2).start()
+
+        partial_v[k] = dot(tokens_v[...], weight_v[k])
+
+        @pl.when(k == 1)
+        def _():
+            filter_load.start()
+            pl.semaphore_wait(barrier, 2 * edge + 1)
+            near_copy(0, 0).start()
+            for d in range(1, edge):
+                greet(round_sem.at[0], place(2 * d), proj)
+
+        first = k < 2 * chunks
+
+        @pl.when(jnp.logical_and(jnp.logical_and(first, k >= 2), lax.rem(k, 2) == 0))
+        def _():
+            near_copy(0, k // 2).start()
+            sum_far(k // 2 - 1)
+
+            @pl.when(jnp.logical_or(EAGER, k <= 4))
+            def _():
+                far_copy(k // 2 - 1).start()
+
+        @pl.when(k == 3)
+        def _():
+            pl.semaphore_wait(round_sem.at[0], edge - 1)
+            greet(round_sem.at[1], place(1), proj)
+
+        @pl.when(k == 5)
+        def _():
+            filter_load.wait()
+            lax.fori_loop(0, chunks, transpose_filters, 0)
+            pl.semaphore_wait(round_sem.at[1], 1)
+            spread(lambda r: filt_send.at[r], lambda r: filt_recv.at[r], filt_send_sem, filt_recv_sem)
+            for copy in table_loads + part_loads:
+                copy.start()
+
+        @pl.when(k == 2 * chunks)
+        def _():
+            sum_far(chunks - 1)
+
+            @pl.when(EAGER)
+            def _():
+                far_copy(chunks - 1).start()
+
+        @pl.when(jnp.logical_and(k >= 2 * chunks, lax.rem(k, 2) == 0))
+        def _():
+            near_copy(1, (k - 2 * chunks) // 2).start()
+
+        return carry
+
+    lax.fori_loop(0, 4 * chunks, project, 0)
+    for copy in part_loads:
         copy.wait()
-    await_bytes(filt_recv, filt_recv_sem)
+
+    def gate(n):
+        near_copy(1, n).wait_recv()
+        far_copy(n).wait_recv()
+        valued = partial_v[2 * chunks + 2 * n + 1] + near_recv[1, n] + far_recv[n]
+        gated = keyed_v[n].astype(F32) * valued
+        gated_v[n] = gated
+        sig_send[n] = gated.T.reshape(seq_count, SUB, rows)
+        spread(
+            lambda r: sig_send.at[n, r], lambda r: sig_recv.at[n, r], sig_send_sem.at[n], sig_recv_sem.at[n]
+        )
+
     flip = (1 - 2 * lax.rem(lax.broadcasted_iota(jnp.int32, (1, 1, block), 2), 2)).astype(F32)
 
     def block_spectra(values):
@@ -230,20 +247,11 @@
         filt_spec[n, 1:, :, block:] = spec[1:, :, block:] + flip * spec[:-1, :, :block]
         return carry
 
-    lax.fori_loop(0, chunks, filter_spectra, 0)
-    for copy in part_loads:
-        copy.wait()
-
-    def gate(n):
-        near_copy(1, n).wait_recv()
-        far_copy(n).wait_recv()
-        valued = own_near[n] + near_recv[1, n] + far_recv[n]
-        gated = keyed_v[n].astype(F32) * valued
-        gated_v[n] = gated
-        sig_send[n] = gated.T.reshape(seq_count, SUB, rows)
-        spread(
-            lambda r: sig_send.at[n, r], lambda r: sig_recv.at[n, r], sig_send_sem.at[n], sig_recv_sem.at[n]
-        )
+    def all_filter_spectra():
+        for copy in table_loads:
+            copy.wait()
+        await_bytes(filt_recv, filt_recv_sem)
+        lax.fori_loop(0, chunks, filter_spectra, 0)
 
     def convolve(n):
         await_bytes(sig_recv.at[n], sig_recv_sem.at[n])
@@ -288,23 +296,30 @@
         out_copy(n).start()
 
     def stage(i, carry):
+        @pl.when(i == SPEC_AT)
+        def _():
+            all_filter_spectra()
+
         @pl.when(i < chunks)
         def _():
             gate(i)
 
+            @pl.when(jnp.logical_and(not EAGER, i + 2 < chunks))
+            def _():
+                far_copy(i + 2).start()
+
         @pl.when(i >= LAG)
         def _():
             convolve(i - LAG)
 
         return carry
 
+    def finish_all(n, carry):
+        finish(n)
+        return carry
+
     lax.fori_loop(0, chunks + LAG, stage, 0)
-
-    def last(n, carry):
-        finish(n)
-        return carry
-
-    lax.fori_loop(0, chunks, last, 0)
+    lax.fori_loop(0, chunks, finish_all, 0)
 
     def drain(n, carry):
         near_copy(0, n).wait_send()
@@ -347,9 +362,9 @@
             pltpu.VMEM((block, 2 * block), BF16),
             pltpu.VMEM((2 * block, block), BF16),
             pltpu.VMEM((2 * block, block), BF16),
+            pltpu.VMEM((4 * chunks, rows, step), F32),
             pltpu.VMEM((2, chunks, rows, step), F32),
-            pltpu.VMEM((2, chunks, rows, step), F32),
-            strip, strip, strip, strip, strip,
+            strip, strip, strip,
             filt_pieces, filt_pieces, pieces, pieces, pieces, pieces,
             pltpu.VMEM((chunks, rows, step), BF16),
             pltpu.VMEM((chunks, blocks, SUB, 2 * block), F32),

time: 76.3 us -> 75.9 us (level); the launches traced: 76.1 us -> 74.7 us
  Pallas kernels: 74.2 us -> 72.8 us
    pallas_call x1, Pallas kernels: 74.2 us -> 72.8 us  [body(): pl.pallas_call(functools.partial(kernel, math.isqrt(seq_count // 2), seq_...]
where the time goes in v3:
time: 75.9 us; the launch traced here: 74.7 us
  Pallas kernels  72.8 us (96%)
  local copies, waits for them, and re-layouts  1.87 us (2%)
    pallas_call x1, Pallas kernels, body(): pl.pallas_call(functools.partial(kernel, math.isqrt(seq_count // 2), seq_...  72.8 us
    unnamed x1, local copies, waits for them, and re-layouts  1.87 us

profile of v3, /device:TPU:0, one launch (start us, length us, event | category | flops | bytes accessed | tf_op | source)
XLA Modules:
  0.0 74.7 jit_solution(14248305973212676758)
XLA Ops:
  0.0 72.8 %shard_map.100 = bf16[256,1024]{1,0:T(8,128)(2,1)} custom-call(bf16[256,2048]{1,0:T(8,128)(2,1)} %tokens_h.1, bf16[2048,4096]{1,0:T(8,128)(2,1)} %weight_h.1, bf16[256,1024]{1,0:T(8,128)(2,1)} %query_h.1, bf16[256,1024]{1,0:T(8,128)(2,1)} %keyed_h.1, f32[256,1024]{1,0:T(8,128)} %filters_h.1, f32[1,1024]{1,0:T(1,128)} %bitcast.1, ...), custom_call_target="tpu_custom_call" | custom-call | tf_op jit(solution)/shard_map/pallas_call | solution.py:350
  72.8 1.9 %copy.12 = bf16[256,1024]{1,0:T(8,128)(2,1)} copy(bf16[256,1024]{1,0:T(8,128)(2,1)} %shard_map.100) | data formatting | bytes 1048576

commit v4 on v3

--- a/solution.py
+++ b/solution.py
@@ -14,9 +14,9 @@
 F32 = jnp.float32
 BF16 = jnp.bfloat16
 SUB = 8
-EAGER = True
-SPEC_AT = 0
-LAG = 4
+EAGER = False
+SPEC_AT = 2
+LAG = 3
 
 
 def odd_tables(block):
@@ -165,9 +165,10 @@
     def project(k, carry):
         weight_load(k).wait()
 
-        @pl.when(k + 2 < 4 * chunks)
-        def _():
-            weight_load(k + 2).start()
+        @pl.when(2 * k + 3 < 4 * chunks)
+        def _():
+            weight_load(2 * k + 2).start()
+            weight_load(2 * k + 3).start()
 
         partial_v[k] = dot(tokens_v[...], weight_v[k])
 

time: 75.9 us -> 76.4 us (level)
  Pallas kernels: 72.8 us -> 74.1 us
    pallas_call x1, Pallas kernels: 72.8 us -> 74.1 us  [body(): pl.pallas_call(functools.partial(kernel, math.isqrt(seq_count // 2), seq_...]
where the time goes in v4:
time: 76.4 us; the launch traced here: 75.9 us
  Pallas kernels  74.1 us (97%)
  local copies, waits for them, and re-layouts  1.87 us (2%)
    pallas_call x1, Pallas kernels, body(): pl.pallas_call(functools.partial(kernel, math.isqrt(seq_count // 2), seq_...  74.1 us
    unnamed x1, local copies, waits for them, and re-layouts  1.87 us

profile of v4, /device:TPU:0, one launch (start us, length us, event | category | flops | bytes accessed | tf_op | source)
XLA Modules:
  0.0 75.9 jit_solution(10937821201324137190)
XLA Ops:
  0.0 74.1 %shard_map.100 = bf16[256,1024]{1,0:T(8,128)(2,1)} custom-call(bf16[256,2048]{1,0:T(8,128)(2,1)} %tokens_h.1, bf16[2048,4096]{1,0:T(8,128)(2,1)} %weight_h.1, bf16[256,1024]{1,0:T(8,128)(2,1)} %query_h.1, bf16[256,1024]{1,0:T(8,128)(2,1)} %keyed_h.1, f32[256,1024]{1,0:T(8,128)} %filters_h.1, f32[1,1024]{1,0:T(1,128)} %bitcast.1, ...), custom_call_target="tpu_custom_call" | custom-call | tf_op jit(solution)/shard_map/pallas_call | solution.py:351
  74.1 1.9 %copy.12 = bf16[256,1024]{1,0:T(8,128)(2,1)} copy(bf16[256,1024]{1,0:T(8,128)(2,1)} %shard_map.100) | data formatting | bytes 1048576

commit v5 on v4

--- a/solution.py
+++ b/solution.py
@@ -16,7 +16,7 @@
 SUB = 8
 EAGER = False
 SPEC_AT = 2
-LAG = 3
+LAG = 2
 
 
 def odd_tables(block):

time: 76.4 us -> 75.5 us (0.988)
  no operation moved by 1% of the time
where the time goes in v5:
time: 75.5 us; the launch traced here: 75.2 us
  Pallas kernels  73.4 us (97%)
  local copies, waits for them, and re-layouts  1.87 us (2%)
    pallas_call x1, Pallas kernels, body(): pl.pallas_call(functools.partial(kernel, math.isqrt(seq_count // 2), seq_...  73.4 us
    unnamed x1, local copies, waits for them, and re-layouts  1.87 us

profile of v5, /device:TPU:0, one launch (start us, length us, event | category | flops | bytes accessed | tf_op | source)
XLA Modules:
  0.0 75.2 jit_solution(441249089215986220)
XLA Ops:
  0.0 73.4 %shard_map.100 = bf16[256,1024]{1,0:T(8,128)(2,1)} custom-call(bf16[256,2048]{1,0:T(8,128)(2,1)} %tokens_h.1, bf16[2048,4096]{1,0:T(8,128)(2,1)} %weight_h.1, bf16[256,1024]{1,0:T(8,128)(2,1)} %query_h.1, bf16[256,1024]{1,0:T(8,128)(2,1)} %keyed_h.1, f32[256,1024]{1,0:T(8,128)} %filters_h.1, f32[1,1024]{1,0:T(1,128)} %bitcast.1, ...), custom_call_target="tpu_custom_call" | custom-call | tf_op jit(solution)/shard_map/pallas_call | solution.py:351
  73.4 1.9 %copy.12 = bf16[256,1024]{1,0:T(8,128)(2,1)} copy(bf16[256,1024]{1,0:T(8,128)(2,1)} %shard_map.100) | data formatting | bytes 1048576

commit v6 on v5

--- a/solution.py
+++ b/solution.py
@@ -15,8 +15,8 @@
 BF16 = jnp.bfloat16
 SUB = 8
 EAGER = False
-SPEC_AT = 2
-LAG = 2
+SPEC_AT = 1
+LAG = 1
 
 
 def odd_tables(block):
@@ -297,10 +297,6 @@
         out_copy(n).start()
 
     def stage(i, carry):
-        @pl.when(i == SPEC_AT)
-        def _():
-            all_filter_spectra()
-
         @pl.when(i < chunks)
         def _():
             gate(i)
@@ -308,6 +304,10 @@
             @pl.when(jnp.logical_and(not EAGER, i + 2 < chunks))
             def _():
                 far_copy(i + 2).start()
+
+        @pl.when(i == SPEC_AT)
+        def _():
+            all_filter_spectra()
 
         @pl.when(i >= LAG)
         def _():

time: 75.5 us -> 76.8 us (1.017)
  Pallas kernels: 73.4 us -> 74.7 us
    pallas_call x1, Pallas kernels: 73.4 us -> 74.7 us  [body(): pl.pallas_call(functools.partial(kernel, math.isqrt(seq_count // 2), seq_...]
where the time goes in v6:
time: 76.8 us; the launch traced here: 76.6 us
  Pallas kernels  74.7 us (97%)
  local copies, waits for them, and re-layouts  1.87 us (2%)
    pallas_call x1, Pallas kernels, body(): pl.pallas_call(functools.partial(kernel, math.isqrt(seq_count // 2), seq_...  74.7 us
    unnamed x1, local copies, waits for them, and re-layouts  1.87 us

profile of v6, /device:TPU:0, one launch (start us, length us, event | category | flops | bytes accessed | tf_op | source)
XLA Modules:
  0.0 76.6 jit_solution(1227611195657890640)
XLA Ops:
  0.0 74.7 %shard_map.100 = bf16[256,1024]{1,0:T(8,128)(2,1)} custom-call(bf16[256,2048]{1,0:T(8,128)(2,1)} %tokens_h.1, bf16[2048,4096]{1,0:T(8,128)(2,1)} %weight_h.1, bf16[256,1024]{1,0:T(8,128)(2,1)} %query_h.1, bf16[256,1024]{1,0:T(8,128)(2,1)} %keyed_h.1, f32[256,1024]{1,0:T(8,128)} %filters_h.1, f32[1,1024]{1,0:T(1,128)} %bitcast.1, ...), custom_call_target="tpu_custom_call" | custom-call | tf_op jit(solution)/shard_map/pallas_call | solution.py:351
  74.7 1.9 %copy.12 = bf16[256,1024]{1,0:T(8,128)(2,1)} copy(bf16[256,1024]{1,0:T(8,128)(2,1)} %shard_map.100) | data formatting | bytes 1048576

commit v7 on v5

--- a/solution.py
+++ b/solution.py
@@ -123,8 +123,8 @@
     greet(barrier, seq, chip_partner)
 
     def spread(source, target, send_sem, recv_sem):
-        def send(d, carry):
-            peer = place(d)
+        def send(i, carry):
+            peer = place(2 * i + 1 - i // (seq_count // 2) * (seq_count - 1))
             pltpu.make_async_remote_copy(
                 src_ref=source(peer), dst_ref=target(seq), send_sem=send_sem, recv_sem=recv_sem,
                 device_id=(peer, proj), device_id_type=MESH,
@@ -132,7 +132,7 @@
             return carry
 
         pltpu.make_async_copy(source(seq), target(seq), recv_sem).start()
-        lax.fori_loop(1, seq_count, send, 0)
+        lax.fori_loop(0, seq_count - 1, send, 0)
 
     def await_bytes(ref, sem):
         pltpu.make_async_copy(ref, ref, sem).wait()

time: 75.5 us -> 74.5 us (0.987)
  Pallas kernels: 73.4 us -> 72.4 us
    pallas_call x1, Pallas kernels: 73.4 us -> 72.4 us  [body(): pl.pallas_call(functools.partial(kernel, math.isqrt(seq_count // 2), seq_...]
where the time goes in v7:
time: 74.5 us; the launch traced here: 74.3 us
  Pallas kernels  72.4 us (97%)
  local copies, waits for them, and re-layouts  1.87 us (3%)
    pallas_call x1, Pallas kernels, body(): pl.pallas_call(functools.partial(kernel, math.isqrt(seq_count // 2), seq_...  72.4 us
    unnamed x1, local copies, waits for them, and re-layouts  1.87 us

profile of v7, /device:TPU:0, one launch (start us, length us, event | category | flops | bytes accessed | tf_op | source)
XLA Modules:
  0.0 74.3 jit_solution(8473935607391032017)
XLA Ops:
  0.0 72.4 %shard_map.100 = bf16[256,1024]{1,0:T(8,128)(2,1)} custom-call(bf16[256,2048]{1,0:T(8,128)(2,1)} %tokens_h.1, bf16[2048,4096]{1,0:T(8,128)(2,1)} %weight_h.1, bf16[256,1024]{1,0:T(8,128)(2,1)} %query_h.1, bf16[256,1024]{1,0:T(8,128)(2,1)} %keyed_h.1, f32[256,1024]{1,0:T(8,128)} %filters_h.1, f32[1,1024]{1,0:T(1,128)} %bitcast.1, ...), custom_call_target="tpu_custom_call" | custom-call | tf_op jit(solution)/shard_map/pallas_call | solution.py:351
  72.5 1.9 %copy.12 = bf16[256,1024]{1,0:T(8,128)(2,1)} copy(bf16[256,1024]{1,0:T(8,128)(2,1)} %shard_map.100) | data formatting | bytes 1048576

commit v8 on v7

--- a/solution.py
+++ b/solution.py
@@ -131,8 +131,8 @@
             ).start()
             return carry
 
+        lax.fori_loop(0, seq_count - 1, send, 0)
         pltpu.make_async_copy(source(seq), target(seq), recv_sem).start()
-        lax.fori_loop(0, seq_count - 1, send, 0)
 
     def await_bytes(ref, sem):
         pltpu.make_async_copy(ref, ref, sem).wait()
@@ -228,11 +228,11 @@
         far_copy(n).wait_recv()
         valued = partial_v[2 * chunks + 2 * n + 1] + near_recv[1, n] + far_recv[n]
         gated = keyed_v[n].astype(F32) * valued
-        gated_v[n] = gated
         sig_send[n] = gated.T.reshape(seq_count, SUB, rows)
         spread(
             lambda r: sig_send.at[n, r], lambda r: sig_recv.at[n, r], sig_send_sem.at[n], sig_recv_sem.at[n]
         )
+        gated_v[n] = gated
 
     flip = (1 - 2 * lax.rem(lax.broadcasted_iota(jnp.int32, (1, 1, block), 2), 2)).astype(F32)
 

time: 74.5 us -> 74.5 us (level)
  no operation moved by 1% of the time
where the time goes in v8:
time: 74.5 us; the launch traced here: 74.3 us
  Pallas kernels  72.4 us (97%)
  local copies, waits for them, and re-layouts  1.87 us (3%)
    pallas_call x1, Pallas kernels, body(): pl.pallas_call(functools.partial(kernel, math.isqrt(seq_count // 2), seq_...  72.4 us
    unnamed x1, local copies, waits for them, and re-layouts  1.87 us

profile of v8, /device:TPU:0, one launch (start us, length us, event | category | flops | bytes accessed | tf_op | source)
XLA Modules:
  0.0 74.3 jit_solution(13808483661686588633)
XLA Ops:
  0.0 72.4 %shard_map.100 = bf16[256,1024]{1,0:T(8,128)(2,1)} custom-call(bf16[256,2048]{1,0:T(8,128)(2,1)} %tokens_h.1, bf16[2048,4096]{1,0:T(8,128)(2,1)} %weight_h.1, bf16[256,1024]{1,0:T(8,128)(2,1)} %query_h.1, bf16[256,1024]{1,0:T(8,128)(2,1)} %keyed_h.1, f32[256,1024]{1,0:T(8,128)} %filters_h.1, f32[1,1024]{1,0:T(1,128)} %bitcast.1, ...), custom_call_target="tpu_custom_call" | custom-call | tf_op jit(solution)/shard_map/pallas_call | solution.py:351
  72.5 1.9 %copy.12 = bf16[256,1024]{1,0:T(8,128)(2,1)} copy(bf16[256,1024]{1,0:T(8,128)(2,1)} %shard_map.100) | data formatting | bytes 1048576
